TPU v7x, 128 devices: a whole 4x4x4 slice. The times are simulated.
128 devices in a mesh: fsdp: 8 (over x_lo, y), ctx: 16 (over z, x_hi, core).
Axes of the slice: x: 4 (x_hi: 2, x_lo: 2; x = x_hi * 2 + x_lo), y: 4, z: 4, core: 2. Of those that a mesh axis runs over, the one named last changes fastest.
Arguments:
- layer_input: float32 [8, 3072, 1024], P('fsdp', 'ctx'), may hold values from -4 to 4
- cotangent: float32 [8, 3072, 1024], P('fsdp', 'ctx'), may hold values from -1.25 to 1.25
- w_qkv: bfloat16 [1024, 3072], P('fsdp'), may hold values from -0.1875 to 0.1875
- b_q: bfloat16 [1024], P('fsdp'), may hold values from -4 to 4
- b_v: bfloat16 [1024], P('fsdp'), may hold values from -0.8984375 to 0.8984375
- w_out: bfloat16 [1024, 1024], P('fsdp'), may hold values from -2 to 2
- b_out: bfloat16 [1024], P('fsdp'), may hold values from -3 to 3
- g_attn: bfloat16 [1024], P('fsdp'), may hold values from 0.099609375 to 1.8984375
- beta_attn: bfloat16 [1024], P('fsdp'), may hold values from -3 to 3
- w_in: bfloat16 [1024, 4096], P('fsdp'), may hold values from -0.1875 to 0.1875
- b_in: bfloat16 [4096], P('fsdp'), may hold values from -3 to 3
- w_back: bfloat16 [4096, 1024], P('fsdp'), may hold values from -0.09375 to 0.09375
- b_back: bfloat16 [1024], P('fsdp'), may hold values from -3 to 3
- g_mlp: bfloat16 [1024], P('fsdp'), may hold values from 0.099609375 to 1.8984375
- beta_mlp: bfloat16 [1024], P('fsdp'), may hold values from -3 to 3
Outputs:
- output: float32 [8, 3072, 1024], P('fsdp', 'ctx')
- grad_input: float32 [8, 3072, 1024], P('fsdp', 'ctx')
- grad_w_qkv: float32 [1024, 3072], P('fsdp')
- grad_b_q: float32 [1024], P('fsdp')
- grad_b_v: float32 [1024], P('fsdp')
- grad_w_out: float32 [1024, 1024], P('fsdp')
- grad_b_out: float32 [1024], P('fsdp')
- grad_g_attn: float32 [1024], P('fsdp')
- grad_beta_attn: float32 [1024], P('fsdp')
- grad_w_in: float32 [1024, 4096], P('fsdp')
- grad_b_in: float32 [4096], P('fsdp')
- grad_w_back: float32 [4096, 1024], P('fsdp')
- grad_b_back: float32 [1024], P('fsdp')
- grad_g_mlp: float32 [1024], P('fsdp')
- grad_beta_mlp: float32 [1024], P('fsdp')
All inputs are finite; a program needn't handle non-finite values.
Results may differ from a plain program's by a relative error of at most 0.025.
Values may be sent and summed in bfloat16 or wider, within the bound.
A program may use at most 192 MiB of HBM per device.

v0:
```python
import math

import jax
import jax.numpy as jnp
from jax import lax
from jax.sharding import PartitionSpec as P

HEADS = 16
HEAD_DIM = 64


EPSILON = 1e-05
ROOT_HALF = 0.7071067811865476
INV_ROOT_TWO_PI = 0.3989422804014327


def passed_along(value, axis, steps):
    count = lax.axis_size(axis)
    pairs = [(source, (source + steps) % count) for source in range(count)]
    return lax.ppermute(value, axis, pairs)


def widened(values):
    return values.astype(jnp.float32)


def layer_norm(hidden, gain, offset):
    center = hidden - jnp.mean(hidden, axis=-1, keepdims=True)
    inverse = lax.rsqrt(jnp.mean(center * center, axis=-1, keepdims=True) + EPSILON)
    normed = center * inverse
    return (normed * gain + offset, normed, inverse)


def norm_back(upstream, normed, inverse, gain):
    scaled = upstream * gain
    return inverse * (
        scaled
        - jnp.mean(scaled, axis=-1, keepdims=True)
        - normed * jnp.mean(scaled * normed, axis=-1, keepdims=True)
    )


def gelu_value(inputs):
    return 0.5 * inputs * (1.0 + jax.scipy.special.erf(inputs * ROOT_HALF))


def gelu_slope(inputs):
    return (
        0.5 * (1.0 + jax.scipy.special.erf(inputs * ROOT_HALF))
        + inputs * jnp.exp(-0.5 * inputs * inputs) * INV_ROOT_TWO_PI
    )


def shards(
    layer_input,
    cotangent,
    w_qkv,
    b_q,
    b_v,
    w_out,
    b_out,
    g_attn,
    beta_attn,
    w_in,
    b_in,
    w_back,
    b_back,
    g_mlp,
    beta_mlp,
):
    width = layer_input.shape[-1]
    scale = 1.0 / math.sqrt(HEAD_DIM)
    params = (
        w_qkv,
        b_q,
        b_v,
        w_out,
        b_out,
        g_attn,
        beta_attn,
        w_in,
        b_in,
        w_back,
        b_back,
        g_mlp,
        beta_mlp,
    )
    gathered = (
        lax.all_gather(params[0], "fsdp", axis=0, tiled=True),
        lax.all_gather(params[1], "fsdp", axis=0, tiled=True),
        lax.all_gather(params[2], "fsdp", axis=0, tiled=True),
        lax.all_gather(params[3], "fsdp", axis=0, tiled=True),
        lax.all_gather(params[4], "fsdp", axis=0, tiled=True),
        lax.all_gather(params[5], "fsdp", axis=0, tiled=True),
        lax.all_gather(params[6], "fsdp", axis=0, tiled=True),
        lax.all_gather(params[7], "fsdp", axis=0, tiled=True),
        lax.all_gather(params[8], "fsdp", axis=0, tiled=True),
        lax.all_gather(params[9], "fsdp", axis=0, tiled=True),
        lax.all_gather(params[10], "fsdp", axis=0, tiled=True),
        lax.all_gather(params[11], "fsdp", axis=0, tiled=True),
        lax.all_gather(params[12], "fsdp", axis=0, tiled=True),
    )
    (
        full_qkv,
        full_bq,
        full_bv,
        full_out,
        full_bout,
        full_gattn,
        full_battn,
        full_in,
        full_bin,
        full_back,
        full_bback,
        full_gmlp,
        full_bmlp,
    ) = gathered
    rows = layer_input.reshape(-1, width)
    local_rows = rows.shape[0]
    rows_low = rows.astype(jnp.bfloat16)
    projected = jnp.dot(rows_low, full_qkv, preferred_element_type=jnp.float32)
    query = ((projected[:, :width] + widened(full_bq)) * scale).astype(jnp.bfloat16)
    keys = projected[:, width : 2 * width].astype(jnp.bfloat16)
    values = (projected[:, 2 * width :] + widened(full_bv)).astype(jnp.bfloat16)
    query_heads = query.reshape(local_rows, HEADS, HEAD_DIM)
    highest = jnp.full((HEADS, local_rows), -1e30, jnp.float32)
    key_heads = lax.all_gather(keys, "ctx", axis=0, tiled=True).reshape(-1, HEADS, HEAD_DIM)
    value_heads = lax.all_gather(values, "ctx", axis=0, tiled=True).reshape(-1, HEADS, HEAD_DIM)
    scores = jnp.einsum("qhd,khd->hqk", query_heads, key_heads, preferred_element_type=jnp.float32)
    fresh = jnp.maximum(highest, jnp.max(scores, axis=-1))
    weights = jnp.exp(scores - fresh[..., None])
    total = jnp.sum(weights, axis=-1)
    accum = jnp.einsum(
        "hqk,khd->hqd",
        weights.astype(jnp.bfloat16),
        value_heads,
        preferred_element_type=jnp.float32,
    )
    highest, total, accum = (fresh, total, accum)
    log_total = highest + jnp.log(total)
    mixed = (
        (accum / total[..., None])
        .transpose(1, 0, 2)
        .reshape(local_rows, width)
        .astype(jnp.bfloat16)
    )
    first_sum = (
        rows + jnp.dot(mixed, full_out, preferred_element_type=jnp.float32) + widened(full_bout)
    )
    first_out, first_normed, first_inverse = layer_norm(
        first_sum, widened(full_gattn), widened(full_battn)
    )
    first_low = first_out.astype(jnp.bfloat16)
    pre_act = jnp.dot(first_low, full_in, preferred_element_type=jnp.float32) + widened(full_bin)
    activated = gelu_value(pre_act).astype(jnp.bfloat16)
    second_sum = (
        first_out
        + jnp.dot(activated, full_back, preferred_element_type=jnp.float32)
        + widened(full_bback)
    )
    output, second_normed, second_inverse = layer_norm(
        second_sum, widened(full_gmlp), widened(full_bmlp)
    )
    again = (
        lax.all_gather(params[0], "fsdp", axis=0, tiled=True),
        lax.all_gather(params[1], "fsdp", axis=0, tiled=True),
        lax.all_gather(params[2], "fsdp", axis=0, tiled=True),
        lax.all_gather(params[3], "fsdp", axis=0, tiled=True),
        lax.all_gather(params[4], "fsdp", axis=0, tiled=True),
        lax.all_gather(params[5], "fsdp", axis=0, tiled=True),
        lax.all_gather(params[6], "fsdp", axis=0, tiled=True),
        lax.all_gather(params[7], "fsdp", axis=0, tiled=True),
        lax.all_gather(params[8], "fsdp", axis=0, tiled=True),
        lax.all_gather(params[9], "fsdp", axis=0, tiled=True),
        lax.all_gather(params[10], "fsdp", axis=0, tiled=True),
        lax.all_gather(params[11], "fsdp", axis=0, tiled=True),
        lax.all_gather(params[12], "fsdp", axis=0, tiled=True),
    )
    back_qkv = again[0]
    back_out = again[3]
    back_gattn = again[5]
    back_in = again[7]
    back_back = again[9]
    back_gmlp = again[11]
    upstream = cotangent.reshape(-1, width)
    grad_g_mlp = jnp.sum(upstream * second_normed, axis=0)
    grad_beta_mlp = jnp.sum(upstream, axis=0)
    grad_second = norm_back(upstream, second_normed, second_inverse, widened(back_gmlp))
    grad_b_back = jnp.sum(grad_second, axis=0)
    grad_second_low = grad_second.astype(jnp.bfloat16)
    grad_w_back = jnp.einsum(
        "tf,td->fd", activated, grad_second_low, preferred_element_type=jnp.float32
    )
    grad_pre = jnp.einsum(
        "td,fd->tf", grad_second_low, back_back, preferred_element_type=jnp.float32
    ) * gelu_slope(pre_act)
    grad_b_in = jnp.sum(grad_pre, axis=0)
    grad_pre_low = grad_pre.astype(jnp.bfloat16)
    grad_w_in = jnp.einsum("td,tf->df", first_low, grad_pre_low, preferred_element_type=jnp.float32)
    grad_first_out = grad_second + jnp.einsum(
        "tf,df->td", grad_pre_low, back_in, preferred_element_type=jnp.float32
    )
    grad_g_attn = jnp.sum(grad_first_out * first_normed, axis=0)
    grad_beta_attn = jnp.sum(grad_first_out, axis=0)
    grad_first = norm_back(grad_first_out, first_normed, first_inverse, widened(back_gattn))
    grad_b_out = jnp.sum(grad_first, axis=0)
    grad_first_low = grad_first.astype(jnp.bfloat16)
    grad_w_out = jnp.einsum("td,te->de", mixed, grad_first_low, preferred_element_type=jnp.float32)
    grad_mixed = jnp.einsum(
        "te,de->td", grad_first_low, back_out, preferred_element_type=jnp.float32
    ).astype(jnp.bfloat16)
    delta = jnp.sum(
        (widened(grad_mixed) * widened(mixed)).reshape(local_rows, HEADS, HEAD_DIM), axis=-1
    ).T
    grad_heads = grad_mixed.reshape(local_rows, HEADS, HEAD_DIM)

    def attend_back(key_block, value_block):
        key_heads = key_block.reshape(-1, HEADS, HEAD_DIM)
        value_heads = value_block.reshape(-1, HEADS, HEAD_DIM)
        scores = jnp.einsum(
            "qhd,khd->hqk", query_heads, key_heads, preferred_element_type=jnp.float32
        )
        prob = jnp.exp(scores - log_total[..., None])
        value_part = jnp.einsum(
            "hqk,qhd->khd",
            prob.astype(jnp.bfloat16),
            grad_heads,
            preferred_element_type=jnp.float32,
        ).reshape(-1, width)
        grad_prob = jnp.einsum(
            "qhd,khd->hqk", grad_heads, value_heads, preferred_element_type=jnp.float32
        )
        grad_scores = (prob * (grad_prob - delta[..., None])).astype(jnp.bfloat16)
        query_part = jnp.einsum(
            "hqk,khd->qhd", grad_scores, key_heads, preferred_element_type=jnp.float32
        )
        key_part = jnp.einsum(
            "hqk,qhd->khd", grad_scores, query_heads, preferred_element_type=jnp.float32
        ).reshape(-1, width)
        return (key_part, value_part, query_part)

    def visit(position, carry):
        key_block, value_block, grad_key_block, grad_value_block, grad_query_acc = carry
        key_part, value_part, query_part = attend_back(key_block, value_block)
        grad_key_block = grad_key_block + key_part
        grad_value_block = grad_value_block + value_part
        grad_query_acc = grad_query_acc + query_part
        key_block, value_block = passed_along((key_block, value_block), "ctx", 1)
        grad_key_block, grad_value_block = (
            passed_along(grad_key_block.astype(jnp.bfloat16), "ctx", 1).astype(
                grad_key_block.dtype
            ),
            passed_along(grad_value_block.astype(jnp.bfloat16), "ctx", 1).astype(
                grad_value_block.dtype
            ),
        )
        return (key_block, value_block, grad_key_block, grad_value_block, grad_query_acc)

    zero_block = jnp.zeros((local_rows, width), jnp.float32)
    start_carry = (
        keys,
        values,
        zero_block,
        zero_block,
        jnp.zeros((local_rows, HEADS, HEAD_DIM), jnp.float32),
    )
    final_carry = lax.fori_loop(0, lax.axis_size("ctx"), visit, start_carry)
    grad_keys = final_carry[2]
    grad_values = final_carry[3]
    grad_query_heads = final_carry[4]
    grad_query = grad_query_heads.reshape(local_rows, width) * scale
    grad_b_q = jnp.sum(grad_query, axis=0)
    grad_b_v = jnp.sum(grad_values, axis=0)
    grad_proj = jnp.concatenate([grad_query, grad_keys, grad_values], axis=1).astype(jnp.bfloat16)
    grad_w_qkv = jnp.einsum("td,te->de", rows_low, grad_proj, preferred_element_type=jnp.float32)
    grad_input = grad_first + jnp.einsum(
        "te,de->td", grad_proj, back_qkv, preferred_element_type=jnp.float32
    )
    gradients = (
        grad_w_qkv,
        grad_b_q,
        grad_b_v,
        grad_w_out,
        grad_b_out,
        grad_g_attn,
        grad_beta_attn,
        grad_w_in,
        grad_b_in,
        grad_w_back,
        grad_b_back,
        grad_g_mlp,
        grad_beta_mlp,
    )
    owned = (
        lax.psum_scatter(
            gradients[0].astype(jnp.bfloat16), "fsdp", scatter_dimension=0, tiled=True
        ).astype(jnp.float32),
        lax.psum_scatter(
            gradients[1].astype(jnp.bfloat16), "fsdp", scatter_dimension=0, tiled=True
        ).astype(jnp.float32),
        lax.psum_scatter(
            gradients[2].astype(jnp.bfloat16), "fsdp", scatter_dimension=0, tiled=True
        ).astype(jnp.float32),
        lax.psum_scatter(
            gradients[3].astype(jnp.bfloat16), "fsdp", scatter_dimension=0, tiled=True
        ).astype(jnp.float32),
        lax.psum_scatter(
            gradients[4].astype(jnp.bfloat16), "fsdp", scatter_dimension=0, tiled=True
        ).astype(jnp.float32),
        lax.psum_scatter(
            gradients[5].astype(jnp.bfloat16), "fsdp", scatter_dimension=0, tiled=True
        ).astype(jnp.float32),
        lax.psum_scatter(
            gradients[6].astype(jnp.bfloat16), "fsdp", scatter_dimension=0, tiled=True
        ).astype(jnp.float32),
        lax.psum_scatter(
            gradients[7].astype(jnp.bfloat16), "fsdp", scatter_dimension=0, tiled=True
        ).astype(jnp.float32),
        lax.psum_scatter(
            gradients[8].astype(jnp.bfloat16), "fsdp", scatter_dimension=0, tiled=True
        ).astype(jnp.float32),
        lax.psum_scatter(
            gradients[9].astype(jnp.bfloat16), "fsdp", scatter_dimension=0, tiled=True
        ).astype(jnp.float32),
        lax.psum_scatter(
            gradients[10].astype(jnp.bfloat16), "fsdp", scatter_dimension=0, tiled=True
        ).astype(jnp.float32),
        lax.psum_scatter(
            gradients[11].astype(jnp.bfloat16), "fsdp", scatter_dimension=0, tiled=True
        ).astype(jnp.float32),
        lax.psum_scatter(
            gradients[12].astype(jnp.bfloat16), "fsdp", scatter_dimension=0, tiled=True
        ).astype(jnp.float32),
    )
    summed = (
        lax.psum(owned[0].astype(jnp.bfloat16), "ctx").astype(jnp.float32),
        lax.psum(owned[1].astype(jnp.bfloat16), "ctx").astype(jnp.float32),
        lax.psum(owned[2].astype(jnp.bfloat16), "ctx").astype(jnp.float32),
        lax.psum(owned[3].astype(jnp.bfloat16), "ctx").astype(jnp.float32),
        lax.psum(owned[4].astype(jnp.bfloat16), "ctx").astype(jnp.float32),
        lax.psum(owned[5].astype(jnp.bfloat16), "ctx").astype(jnp.float32),
        lax.psum(owned[6].astype(jnp.bfloat16), "ctx").astype(jnp.float32),
        lax.psum(owned[7].astype(jnp.bfloat16), "ctx").astype(jnp.float32),
        lax.psum(owned[8].astype(jnp.bfloat16), "ctx").astype(jnp.float32),
        lax.psum(owned[9].astype(jnp.bfloat16), "ctx").astype(jnp.float32),
        lax.psum(owned[10].astype(jnp.bfloat16), "ctx").astype(jnp.float32),
        lax.psum(owned[11].astype(jnp.bfloat16), "ctx").astype(jnp.float32),
        lax.psum(owned[12].astype(jnp.bfloat16), "ctx").astype(jnp.float32),
    )
    return (output.reshape(layer_input.shape), grad_input.reshape(layer_input.shape)) + tuple(
        summed
    )


def solution(mesh):
    return jax.shard_map(
        shards,
        mesh=mesh,
        in_specs=(
            P("fsdp", "ctx", None),
            P("fsdp", "ctx", None),
            P("fsdp", None),
            P("fsdp"),
            P("fsdp"),
            P("fsdp", None),
            P("fsdp"),
            P("fsdp"),
            P("fsdp"),
            P("fsdp", None),
            P("fsdp"),
            P("fsdp", None),
            P("fsdp"),
            P("fsdp"),
            P("fsdp"),
        ),
        out_specs=(
            P("fsdp", "ctx", None),
            P("fsdp", "ctx", None),
            P("fsdp", None),
            P("fsdp"),
            P("fsdp"),
            P("fsdp", None),
            P("fsdp"),
            P("fsdp"),
            P("fsdp"),
            P("fsdp", None),
            P("fsdp"),
            P("fsdp", None),
            P("fsdp"),
            P("fsdp"),
            P("fsdp"),
        ),
        check_vma=False,
    )
```

profile of v0, /device:TPU:1, one launch (start us, length us, event | category | flops | bytes accessed | tf_op | source)
XLA Modules:
  0.0 1607.7 jit_solution(413708523609790628)
XLA Ops:
  8.0 77.2 %all-gather.16.cloned.1.call-done = bf16[1024,3072]{1,0:T(8,128)(2,1)} async-done(((bf16[128,3072]{1,0:T(8,128)(2,1)}), bf16[1024,3072]{1,0:T(8,128)(2,1)}) %all-gather.16.cloned.1.call-update) | async-done | bytes 6291472 | tf_op jit(solution)/shard_map/all_gather | solution.py:89
  90.6 12.2 all-gather
  102.8 12.5 all-gather.1
  118.0 13.6 all-gather.2
  131.7 12.3 all-gather.3
  144.0 13.4 all-gather.4
  157.4 19.5 %all-gather.5 = bf16[8,1,512]{2,1,0:T(2,128)(2,1)S(1)} all-gather(bf16[1,1,512]{2,1,0:T(2,128)(2,1)S(1)} %reshape.151), channel_id=1, replica_groups=mesh['fsdp'=8,'ctx'=16] {'fsdp'}, dimensions={0}, use_global_device_ids=true | all-gather | bytes 9216 | tf_op jit(solution)/shard_map/all_gather | solution.py:97
  176.9 11.6 all-gather.6
  188.5 13.7 all-gather.7
  202.2 12.3 all-gather.8
  215.2 8.6 copy.49
  223.9 8.6 copy.50
  232.4 16.9 %fusion.46 = (f32[16,192]{1,0:T(8,128)S(1)}, f32[16,192,3072]{2,1,0:T(8,128)}) fusion(bf16[192,16,64]{0,2,1:T(8,128)(2,1)S(1)} %bitcast.144, bf16[3072,16,64]{0,2,1:T(8,128)(2,1)} %bitcast.147), kind=kOutput, calls=%fused_computation.90 | convolution fusion | flops 1217393664 | bytes 44445696 | tf_op jit(solution)/shard_map/qhd,khd->hqk/dot_general | solution.py:129
  249.4 16.0 fusion.7
  265.4 14.8 divide_convert_fusion
  283.9 68.3 %all-gather.24.cloned.1.call-done = bf16[1024,4096]{1,0:T(8,128)(2,1)} async-done(((bf16[128,4096]{1,0:T(8,128)(2,1)}), bf16[1024,4096]{1,0:T(8,128)(2,1)}) %all-gather.24.cloned.1.call-update) | async-done | bytes 8388624 | tf_op jit(solution)/shard_map/all_gather | solution.py:96
  352.2 6.9 convolution_add_fusion
  359.1 85.3 %all-gather.26.cloned.1.call-done = bf16[4096,1024]{1,0:T(8,128)(2,1)} async-done(((bf16[512,1024]{1,0:T(8,128)(2,1)}), bf16[4096,1024]{1,0:T(8,128)(2,1)}) %all-gather.26.cloned.1.call-update) | async-done | bytes 8388624 | tf_op jit(solution)/shard_map/all_gather | solution.py:98
  444.4 6.4 fusion.48
  466.0 634.1 %while.19 = (s32[]{:T(128)}, bf16[192,1024]{0,1:T(8,128)(2,1)S(1)}, bf16[192,1024]{0,1:T(8,128)(2,1)S(1)}, f32[192,1024]{0,1:T(8,128)}, f32[192,1024]{0,1:T(8,12...) while((s32[]{:T(128)}, bf16[192,1024]{0,1:T(8,128)(2,1)S(1)}, ...), condition=%wide.region_12.0_spmd.clone, body=%wide.region_11.0_spmd.clone.sunk | while | flops 382992384 | bytes 43291048 | solution.py:267
  1006.6 7.6 collective-permute-done.2
  1046.5 8.9 collective-permute-done.2
  1086.4 10.1 collective-permute-done.2
  1109.0 8.6 copy.57
  1121.1 7.6 convolution_convert_fusion
  1136.2 72.8 %reduce-scatter.13.cloned.1.call-done = bf16[128,3072]{1,0:T(8,128)(2,1)} async-done(((bf16[1024,3072]{1,0:T(8,128)(2,1)}), bf16[128,3072]{1,0:T(8,128)(2,1)}) %reduce-scatter.13.cloned.1.call-update) | async-done | bytes 786448
  1211.3 37.0 %reduce-scatter.7.cloned.1.call-done = bf16[128,1024]{1,0:T(8,128)(2,1)} async-done(((bf16[1024,1024]{1,0:T(8,128)(2,1)}), bf16[128,1024]{1,0:T(8,128)(2,1)}) %reduce-scatter.7.cloned.1.call-update) | async-done | bytes 262160 | tf_op jit(solution)/shard_map/reduce_scatter | solution.py:304
  1248.3 99.0 %reduce-scatter.11.cloned.1.call-done = bf16[512,1024]{1,0:T(8,128)(2,1)} async-done(((bf16[4096,1024]{1,0:T(8,128)(2,1)}), bf16[512,1024]{1,0:T(8,128)(2,1)}) %reduce-scatter.11.cloned.1.call-update) | async-done | bytes 1048592 | tf_op jit(solution)/shard_map/reduce_scatter | solution.py:322
  1347.3 93.8 %reduce-scatter.9.cloned.1.call-done = bf16[128,4096]{1,0:T(8,128)(2,1)} async-done(((bf16[1024,4096]{1,0:T(8,128)(2,1)}), bf16[128,4096]{1,0:T(8,128)(2,1)}) %reduce-scatter.9.cloned.1.call-update) | async-done | bytes 1048592 | tf_op jit(solution)/shard_map/reduce_scatter | solution.py:316
  1443.2 24.9 %all-reduce.11 = (bf16[1024]{0:T(1024)(128)(2,1)S(1)}, bf16[1024]{0:T(1024)(128)(2,1)S(1)}, bf16[1024]{0:T(1024)(128)(2,1)S(1)}, bf16[1024]{0:T(1024)(128)(2,1)S...) all-reduce(bf16[1024]{0:T(1024)(128)(2,1)S(1)} %convert_element_typ, ...), channel_id=3, replica_groups=mesh['fsdp'=8,'ctx'=16] {'fsdp'}, use_global_device_ids=true, to_apply=%region_16.0.clone | all-reduce | flops 12288 | bytes 49152
  1468.7 40.1 %all-reduce.9 = (bf16[128]{0:T(256)(128)(2,1)S(1)}, bf16[128]{0:T(256)(128)(2,1)S(1)}, bf16[128]{0:T(256)(128)(2,1)S(1)}, bf16[128]{0:T(256)(128)(2,1)S(1)}, bf1...) all-reduce(bf16[128]{0:T(256)(128)(2,1)S(1)} %dynamic-slice.1, ...), channel_id=1, replica_groups=mesh['fsdp'=8,'ctx'=16] {'ctx'}, use_global_device_ids=true, to_apply=%region_17.0 | all-reduce | flops 1536 | bytes 6144 | tf_op jit(solution)/shard_map/psum | solution.py:337
  1519.4 74.5 %all-reduce.14.cloned.1.call-done = (bf16[128,3072]{0,1:T(8,128)(2,1)}, bf16[128,1024]{1,0:T(8,128)(2,1)}, bf16[128,4096]{1,0:T(8,128)(2,1)}, bf16[512,1024]{1,0:T(8,128)(2,1)}) async-done(((bf16[128,3072]{0,1:T(8,128)(2,1)}, bf16[128,1024]{1,0:T(8,128)(2,1)}, bf16[128,4096]{1,0:T(8,128)(2,1)}, bf16[512,1024]{1,0:T(8,128)(2,1)}), (bf16[128,3072]{0,1:T(8,128)(2,1)}, bf16[128,1024]{1,0:T(8,128)(2,1)}, ...) | async-done | bytes 3145744 | tf_op jit(solution)/shard_map/psum | solution.py:336
  (651 shorter events, 675.3 us)
Async XLA Ops:
  7.2 78.0 %all-gather.16.cloned.1.call-start = ((), (), s32[]{:S(2)}) async-start(), calls=%async_computation.4 | async-start | bytes 7077888 | tf_op jit(solution)/shard_map/all_gather | solution.py:89
  7.9 207.3 %all-gather.18.cloned.1.call-start = ((), (), s32[]{:S(2)}) async-start(), calls=%async_computation.5 | async-start | bytes 6684672 | tf_op jit(solution)/shard_map/all_gather | solution.py:127
  90.5 133.3 %all-gather.20.cloned.1.call-start = ((), (), s32[]{:S(2)}) async-start(), calls=%async_computation.6 | async-start | bytes 6684672 | tf_op jit(solution)/shard_map/all_gather | solution.py:128
  116.2 164.9 %all-gather.22.cloned.1.call-start = ((), (), s32[]{:S(2)}) async-start(), calls=%async_computation.7 | async-start | bytes 2359296 | tf_op jit(solution)/shard_map/all_gather | solution.py:92
  116.8 235.4 %all-gather.24.cloned.1.call-start = ((), (), s32[]{:S(2)}) async-start(), calls=%async_computation.8 | async-start | bytes 9437184 | tf_op jit(solution)/shard_map/all_gather | solution.py:96
  117.4 327.0 %all-gather.26.cloned.1.call-start = ((), (), s32[]{:S(2)}) async-start(), calls=%async_computation.9 | async-start | bytes 9437184 | tf_op jit(solution)/shard_map/all_gather | solution.py:98
  118.0 1091.0 %reduce-scatter.13.cloned.1.call-start = ((), (), s32[]{:S(2)}) async-start(), calls=%async_computation.13 | async-start | bytes 7077888
  484.4 19.3 %collective-permute-start.1 = (bf16[192,1024]{0,1:T(8,128)(2,1)}, bf16[192,1024]{0,1:T(8,128)(2,1)S(1)}, u32[]{:S(2)}, u32[]{:S(2)}) collective-permute-start(bf16[192,1024]{0,1:T(8,128)(2,1)} %copy.67), channel_id=1, source_target_pairs={{0,1},{1,2},{2,3},{3,4},{4,5},{5,6},{6,7},{7,8},{8,9},{9,10},{10,1... | collective-permute-start | bytes 1179656 | tf_op jit(solution)/shard_map/while/body/eval_jaxpr/ppermute | solution.py:20
  524.3 18.4 %collective-permute-start.1 = (bf16[192,1024]{0,1:T(8,128)(2,1)}, bf16[192,1024]{0,1:T(8,128)(2,1)S(1)}, u32[]{:S(2)}, u32[]{:S(2)}) collective-permute-start(bf16[192,1024]{0,1:T(8,128)(2,1)} %copy.67), channel_id=1, source_target_pairs={{0,1},{1,2},{2,3},{3,4},{4,5},{5,6},{6,7},{7,8},{8,9},{9,10},{10,1... | collective-permute-start | bytes 1179656 | tf_op jit(solution)/shard_map/while/body/eval_jaxpr/ppermute | solution.py:20
  749.5 18.1 %collective-permute-start.2 = (bf16[192,1024]{0,1:T(8,128)(2,1)}, bf16[192,1024]{0,1:T(8,128)(2,1)}, u32[]{:S(2)}, u32[]{:S(2)}) collective-permute-start(bf16[192,1024]{0,1:T(8,128)(2,1)} %fusion.113), channel_id=1, source_target_pairs={{0,1},{1,2},{2,3},{3,4},{4,5},{5,6},{6,7},{7,8},{8,9},{9,10},{10,1... | collective-permute-start | bytes 1179656 | tf_op jit(solution)/shard_map/while/body/eval_jaxpr/ppermute | solution.py:20
  788.5 20.2 %collective-permute-start.2 = (bf16[192,1024]{0,1:T(8,128)(2,1)}, bf16[192,1024]{0,1:T(8,128)(2,1)}, u32[]{:S(2)}, u32[]{:S(2)}) collective-permute-start(bf16[192,1024]{0,1:T(8,128)(2,1)} %fusion.113), channel_id=1, source_target_pairs={{0,1},{1,2},{2,3},{3,4},{4,5},{5,6},{6,7},{7,8},{8,9},{9,10},{10,1... | collective-permute-start | bytes 1179656 | tf_op jit(solution)/shard_map/while/body/eval_jaxpr/ppermute | solution.py:20
  828.1 21.8 %collective-permute-start.2 = (bf16[192,1024]{0,1:T(8,128)(2,1)}, bf16[192,1024]{0,1:T(8,128)(2,1)}, u32[]{:S(2)}, u32[]{:S(2)}) collective-permute-start(bf16[192,1024]{0,1:T(8,128)(2,1)} %fusion.113), channel_id=1, source_target_pairs={{0,1},{1,2},{2,3},{3,4},{4,5},{5,6},{6,7},{7,8},{8,9},{9,10},{10,1... | collective-permute-start | bytes 1179656 | tf_op jit(solution)/shard_map/while/body/eval_jaxpr/ppermute | solution.py:20
  833.9 18.1 %collective-permute-start.3 = (bf16[192,1024]{0,1:T(8,128)(2,1)S(1)}, bf16[192,1024]{0,1:T(8,128)(2,1)S(1)}, u32[]{:S(2)}, u32[]{:S(2)}) collective-permute-start(bf16[192,1024]{0,1:T(8,128)(2,1)S(1)} %fusion.115), channel_id=1, source_target_pairs={{0,1},{1,2},{2,3},{3,4},{4,5},{5,6},{6,7},{7,8},{8,9},{9,10},{10,1... | collective-permute-start | bytes 1179656 | tf_op jit(solution)/shard_map/while/body/eval_jaxpr/ppermute | solution.py:20
  867.9 23.0 %collective-permute-start.2 = (bf16[192,1024]{0,1:T(8,128)(2,1)}, bf16[192,1024]{0,1:T(8,128)(2,1)}, u32[]{:S(2)}, u32[]{:S(2)}) collective-permute-start(bf16[192,1024]{0,1:T(8,128)(2,1)} %fusion.113), channel_id=1, source_target_pairs={{0,1},{1,2},{2,3},{3,4},{4,5},{5,6},{6,7},{7,8},{8,9},{9,10},{10,1... | collective-permute-start | bytes 1179656 | tf_op jit(solution)/shard_map/while/body/eval_jaxpr/ppermute | solution.py:20
  873.8 19.3 %collective-permute-start.3 = (bf16[192,1024]{0,1:T(8,128)(2,1)S(1)}, bf16[192,1024]{0,1:T(8,128)(2,1)S(1)}, u32[]{:S(2)}, u32[]{:S(2)}) collective-permute-start(bf16[192,1024]{0,1:T(8,128)(2,1)S(1)} %fusion.115), channel_id=1, source_target_pairs={{0,1},{1,2},{2,3},{3,4},{4,5},{5,6},{6,7},{7,8},{8,9},{9,10},{10,1... | collective-permute-start | bytes 1179656 | tf_op jit(solution)/shard_map/while/body/eval_jaxpr/ppermute | solution.py:20
  907.8 24.2 %collective-permute-start.2 = (bf16[192,1024]{0,1:T(8,128)(2,1)}, bf16[192,1024]{0,1:T(8,128)(2,1)}, u32[]{:S(2)}, u32[]{:S(2)}) collective-permute-start(bf16[192,1024]{0,1:T(8,128)(2,1)} %fusion.113), channel_id=1, source_target_pairs={{0,1},{1,2},{2,3},{3,4},{4,5},{5,6},{6,7},{7,8},{8,9},{9,10},{10,1... | collective-permute-start | bytes 1179656 | tf_op jit(solution)/shard_map/while/body/eval_jaxpr/ppermute | solution.py:20
  913.6 20.5 %collective-permute-start.3 = (bf16[192,1024]{0,1:T(8,128)(2,1)S(1)}, bf16[192,1024]{0,1:T(8,128)(2,1)S(1)}, u32[]{:S(2)}, u32[]{:S(2)}) collective-permute-start(bf16[192,1024]{0,1:T(8,128)(2,1)S(1)} %fusion.115), channel_id=1, source_target_pairs={{0,1},{1,2},{2,3},{3,4},{4,5},{5,6},{6,7},{7,8},{8,9},{9,10},{10,1... | collective-permute-start | bytes 1179656 | tf_op jit(solution)/shard_map/while/body/eval_jaxpr/ppermute | solution.py:20
  947.7 25.4 %collective-permute-start.2 = (bf16[192,1024]{0,1:T(8,128)(2,1)}, bf16[192,1024]{0,1:T(8,128)(2,1)}, u32[]{:S(2)}, u32[]{:S(2)}) collective-permute-start(bf16[192,1024]{0,1:T(8,128)(2,1)} %fusion.113), channel_id=1, source_target_pairs={{0,1},{1,2},{2,3},{3,4},{4,5},{5,6},{6,7},{7,8},{8,9},{9,10},{10,1... | collective-permute-start | bytes 1179656 | tf_op jit(solution)/shard_map/while/body/eval_jaxpr/ppermute | solution.py:20
  953.5 21.7 %collective-permute-start.3 = (bf16[192,1024]{0,1:T(8,128)(2,1)S(1)}, bf16[192,1024]{0,1:T(8,128)(2,1)S(1)}, u32[]{:S(2)}, u32[]{:S(2)}) collective-permute-start(bf16[192,1024]{0,1:T(8,128)(2,1)S(1)} %fusion.115), channel_id=1, source_target_pairs={{0,1},{1,2},{2,3},{3,4},{4,5},{5,6},{6,7},{7,8},{8,9},{9,10},{10,1... | collective-permute-start | bytes 1179656 | tf_op jit(solution)/shard_map/while/body/eval_jaxpr/ppermute | solution.py:20
  988.3 25.9 %collective-permute-start.2 = (bf16[192,1024]{0,1:T(8,128)(2,1)}, bf16[192,1024]{0,1:T(8,128)(2,1)}, u32[]{:S(2)}, u32[]{:S(2)}) collective-permute-start(bf16[192,1024]{0,1:T(8,128)(2,1)} %fusion.113), channel_id=1, source_target_pairs={{0,1},{1,2},{2,3},{3,4},{4,5},{5,6},{6,7},{7,8},{8,9},{9,10},{10,1... | collective-permute-start | bytes 1179656 | tf_op jit(solution)/shard_map/while/body/eval_jaxpr/ppermute | solution.py:20
  993.4 22.9 %collective-permute-start.3 = (bf16[192,1024]{0,1:T(8,128)(2,1)S(1)}, bf16[192,1024]{0,1:T(8,128)(2,1)S(1)}, u32[]{:S(2)}, u32[]{:S(2)}) collective-permute-start(bf16[192,1024]{0,1:T(8,128)(2,1)S(1)} %fusion.115), channel_id=1, source_target_pairs={{0,1},{1,2},{2,3},{3,4},{4,5},{5,6},{6,7},{7,8},{8,9},{9,10},{10,1... | collective-permute-start | bytes 1179656 | tf_op jit(solution)/shard_map/while/body/eval_jaxpr/ppermute | solution.py:20
  998.2 19.2 %collective-permute-start = (bf16[192,1024]{0,1:T(8,128)(2,1)}, bf16[192,1024]{0,1:T(8,128)(2,1)S(1)}, u32[]{:S(2)}, u32[]{:S(2)}) collective-permute-start(bf16[192,1024]{0,1:T(8,128)(2,1)} %copy.66), channel_id=1, source_target_pairs={{0,1},{1,2},{2,3},{3,4},{4,5},{5,6},{6,7},{7,8},{8,9},{9,10},{10,1... | collective-permute-start | bytes 1179656 | tf_op jit(solution)/shard_map/while/body/eval_jaxpr/ppermute | solution.py:20
  1029.4 25.9 %collective-permute-start.2 = (bf16[192,1024]{0,1:T(8,128)(2,1)}, bf16[192,1024]{0,1:T(8,128)(2,1)}, u32[]{:S(2)}, u32[]{:S(2)}) collective-permute-start(bf16[192,1024]{0,1:T(8,128)(2,1)} %fusion.113), channel_id=1, source_target_pairs={{0,1},{1,2},{2,3},{3,4},{4,5},{5,6},{6,7},{7,8},{8,9},{9,10},{10,1... | collective-permute-start | bytes 1179656 | tf_op jit(solution)/shard_map/while/body/eval_jaxpr/ppermute | solution.py:20
  1033.3 24.1 %collective-permute-start.3 = (bf16[192,1024]{0,1:T(8,128)(2,1)S(1)}, bf16[192,1024]{0,1:T(8,128)(2,1)S(1)}, u32[]{:S(2)}, u32[]{:S(2)}) collective-permute-start(bf16[192,1024]{0,1:T(8,128)(2,1)S(1)} %fusion.115), channel_id=1, source_target_pairs={{0,1},{1,2},{2,3},{3,4},{4,5},{5,6},{6,7},{7,8},{8,9},{9,10},{10,1... | collective-permute-start | bytes 1179656 | tf_op jit(solution)/shard_map/while/body/eval_jaxpr/ppermute | solution.py:20
  1038.1 20.4 %collective-permute-start = (bf16[192,1024]{0,1:T(8,128)(2,1)}, bf16[192,1024]{0,1:T(8,128)(2,1)S(1)}, u32[]{:S(2)}, u32[]{:S(2)}) collective-permute-start(bf16[192,1024]{0,1:T(8,128)(2,1)} %copy.66), channel_id=1, source_target_pairs={{0,1},{1,2},{2,3},{3,4},{4,5},{5,6},{6,7},{7,8},{8,9},{9,10},{10,1... | collective-permute-start | bytes 1179656 | tf_op jit(solution)/shard_map/while/body/eval_jaxpr/ppermute | solution.py:20
  1070.5 25.9 %collective-permute-start.2 = (bf16[192,1024]{0,1:T(8,128)(2,1)}, bf16[192,1024]{0,1:T(8,128)(2,1)}, u32[]{:S(2)}, u32[]{:S(2)}) collective-permute-start(bf16[192,1024]{0,1:T(8,128)(2,1)} %fusion.113), channel_id=1, source_target_pairs={{0,1},{1,2},{2,3},{3,4},{4,5},{5,6},{6,7},{7,8},{8,9},{9,10},{10,1... | collective-permute-start | bytes 1179656 | tf_op jit(solution)/shard_map/while/body/eval_jaxpr/ppermute | solution.py:20
  1073.2 25.3 %collective-permute-start.3 = (bf16[192,1024]{0,1:T(8,128)(2,1)S(1)}, bf16[192,1024]{0,1:T(8,128)(2,1)S(1)}, u32[]{:S(2)}, u32[]{:S(2)}) collective-permute-start(bf16[192,1024]{0,1:T(8,128)(2,1)S(1)} %fusion.115), channel_id=1, source_target_pairs={{0,1},{1,2},{2,3},{3,4},{4,5},{5,6},{6,7},{7,8},{8,9},{9,10},{10,1... | collective-permute-start | bytes 1179656 | tf_op jit(solution)/shard_map/while/body/eval_jaxpr/ppermute | solution.py:20
  1078.0 21.6 %collective-permute-start = (bf16[192,1024]{0,1:T(8,128)(2,1)}, bf16[192,1024]{0,1:T(8,128)(2,1)S(1)}, u32[]{:S(2)}, u32[]{:S(2)}) collective-permute-start(bf16[192,1024]{0,1:T(8,128)(2,1)} %copy.66), channel_id=1, source_target_pairs={{0,1},{1,2},{2,3},{3,4},{4,5},{5,6},{6,7},{7,8},{8,9},{9,10},{10,1... | collective-permute-start | bytes 1179656 | tf_op jit(solution)/shard_map/while/body/eval_jaxpr/ppermute | solution.py:20
  1117.7 130.5 %reduce-scatter.7.cloned.1.call-start = ((), (), s32[]{:S(2)}) async-start(), calls=%async_computation.10 | async-start | bytes 2359296 | tf_op jit(solution)/shard_map/reduce_scatter | solution.py:304
  1121.0 226.3 %reduce-scatter.11.cloned.1.call-start = ((), (), s32[]{:S(2)}) async-start(), calls=%async_computation.12 | async-start | bytes 9437184 | tf_op jit(solution)/shard_map/reduce_scatter | solution.py:322
  1128.7 312.3 %reduce-scatter.9.cloned.1.call-start = ((), (), s32[]{:S(2)}) async-start(), calls=%async_computation.11 | async-start | bytes 9437184 | tf_op jit(solution)/shard_map/reduce_scatter | solution.py:316
  1136.1 457.8 %all-reduce.14.cloned.1.call-start = ((), (), s32[]{:S(2)}) async-start(), calls=%async_computation.14 | async-start | bytes 6291456 | tf_op jit(solution)/shard_map/psum | solution.py:336
  (167 other events, 3994.5 us)
Sparse Core Ops, SparseCore 0:
  9.7 75.4 all-gather.15
  90.6 63.4 all-gather.17
  157.2 61.9 all-gather.19
  220.7 33.6 all-gather.21
  255.8 96.3 all-gather.23
  353.7 90.6 all-gather.25
  1117.8 91.0 reduce-scatter.12
  1212.0 36.2 reduce-scatter.6
  1250.7 96.5 reduce-scatter.10
  1349.5 91.4 reduce-scatter.8
  1444.4 149.5 all-reduce.13
where the time goes:
time: 1620 us; the launch traced here: 1610 us
  waiting for transfers between devices  743 us (46%)
  matrix products  273 us (17%)
  blocking collectives  186 us (11%)
  starting transfers between devices  175 us (11%)
  other arithmetic  128 us (8%)
  local copies, waits for them, and re-layouts  85.1 us (5%)
  between operations  16.3 us (1%)
    ppermute x64, starting transfers between devices, passed_along(): return lax.ppermute(value, axis, pairs)  174 us
    ppermute x64, waiting for transfers between devices, passed_along(): return lax.ppermute(value, axis, pairs)  133 us
    reduce_scatter x1, waiting for transfers between devices, shards(): lax.psum_scatter(gradients[9].astype(jnp.bfloat16), 'fsdp', scatter_dimen...  99 us
    reduce_scatter x1, waiting for transfers between devices, shards(): lax.psum_scatter(gradients[7].astype(jnp.bfloat16), 'fsdp', scatter_dimen...  93.8 us
    all_gather x1, waiting for transfers between devices, shards(): lax.all_gather(params[9], 'fsdp', axis=0, tiled=True)  85.3 us
    all_gather x1, waiting for transfers between devices, shards(): lax.all_gather(params[0], 'fsdp', axis=0, tiled=True)  77.2 us
    unnamed x12, waiting for transfers between devices  75.2 us
    psum x1, waiting for transfers between devices, shards(): lax.psum(owned[0].astype(jnp.bfloat16), 'ctx').astype(jnp.float32)  74.5 us
  transfers between devices with their start and end apart: 75, of which 44 were waited for; matrix products, arithmetic and copies ran while one was open for 15% of the time, Pallas kernels for 0%

commit v1 on v0

v1 whole, which is shorter than its diff:
```python
import functools
import math

import jax
import jax.numpy as jnp
from jax import lax
from jax.experimental import pallas as pl
from jax.experimental.pallas import tpu as pltpu
from jax.sharding import PartitionSpec as P

HEADS = 16
HEAD_DIM = 64
EPSILON = 1e-05
ROOT_HALF = 0.7071067811865476
INV_ROOT_TWO_PI = 0.3989422804014327
BF16 = jnp.bfloat16
F32 = jnp.float32
MESH = pl.DeviceIdType.MESH
UNITS = 12
MIB = 2**20


def place():
    fsdp, ctx = lax.axis_index("fsdp"), lax.axis_index("ctx")
    return (lax.rem(ctx // 2, 2) * 2 + fsdp // 4, lax.rem(fsdp, 4), ctx // 4, lax.rem(ctx, 2))


def device_at(x, y, z, core):
    x, y, z, core = (lax.rem(x + 4, 4), lax.rem(y + 4, 4), lax.rem(z + 4, 4), lax.rem(core, 2))
    return {"fsdp": lax.rem(x, 2) * 4 + y, "ctx": z * 4 + (x // 2) * 2 + core}


def greet(devices):
    barrier = pltpu.get_barrier_semaphore()
    for device in devices:
        pl.semaphore_signal(barrier, inc=1, device_id=device, device_id_type=MESH)
    pl.semaphore_wait(barrier, len(devices))


def remote(src, dst, send, recv, device):
    return pltpu.make_async_remote_copy(
        src_ref=src, dst_ref=dst, send_sem=send, recv_sem=recv, device_id=device, device_id_type=MESH
    )


GROUPS = 6


def gather_kernel(pk, small, full, smalls, own_sem, y_s, y_r, x_s, x_r, c_s, c_r, s_s, s_r):
    x, y, z, core = place()
    low = lax.rem(x, 2)
    shard = low * 4 + y
    per = UNITS // GROUPS
    half = per // 2
    rows = pl.ds(pl.multiple_of(core * 64, 64), 64)
    sibling = device_at(x, y, z, core + 1)
    ys = {d: device_at(x, y + d, z, core) for d in (1, 2, 3)}
    xs = [device_at(x + 1, y, z, core), device_at(x - 1, y, z, core)]
    across = {(a, d): device_at(x + a, y + d, z, core) for a in (0, 1) for d in range(4) if (a, d) != (0, 0)}
    greet([sibling] + xs + list(ys.values()) + [device_at(x - 1, y - d, z, core) for d in (1, 2, 3)])

    own = pltpu.make_async_copy(pk, full.at[:, shard], own_sem.at[0])
    own.start()
    own_small = pltpu.make_async_copy(small, smalls.at[shard], own_sem.at[1])
    own_small.start()
    small_copies = []
    for i, device in enumerate(across.values()):
        copy = remote(small, smalls.at[shard], s_s.at[i], s_r.at[i], device)
        copy.start()
        small_copies.append(copy)

    def y_copy(g, d):
        units = pl.ds(g * per, per)
        return remote(pk.at[units, rows], full.at[units, shard, rows], y_s.at[g, d - 1], y_r.at[g, d - 1], ys[d])

    def x_copy(g, e, way):
        units = pl.ds(g * per + way * half, half)
        block = low * 4 + lax.rem(y - e + 4, 4)
        src = pk.at[units, rows] if e == 0 else full.at[units, block, rows]
        return remote(src, full.at[units, block, rows], x_s.at[g, e, way], x_r.at[g, e, way], xs[way])

    def c_copy(g, which):
        if which < 3:
            block = low * 4 + lax.rem(y - which + 3, 4)
            units = pl.ds(g * per, per)
        else:
            e, way = (which - 3) // 2, (which - 3) % 2
            block = (1 - low) * 4 + lax.rem(y - e + 4, 4)
            units = pl.ds(g * per + way * half, half)
        ref = full.at[units, block, rows]
        return remote(ref, ref, c_s.at[g, which], c_r.at[g, which], sibling)

    def first(g, _):
        for d in (1, 3, 2):
            y_copy(g, d).start()
        for way in (0, 1):
            x_copy(g, 0, way).start()
        return 0

    def second(g, _):
        for d in (1, 3, 2):
            y_copy(g, d).wait_recv()
            for way in (0, 1):
                x_copy(g, d, way).start()
            c_copy(g, d - 1).start()
        for way in (0, 1):
            x_copy(g, 0, way).wait_recv()
            c_copy(g, 3 + way).start()
        return 0

    def third(g, _):
        for e in (1, 3, 2):
            for way in (0, 1):
                x_copy(g, e, way).wait_recv()
                c_copy(g, 3 + 2 * e + way).start()
        return 0

    def last(g, _):
        for d in (1, 2, 3):
            y_copy(g, d).wait_send()
        for e in range(4):
            for way in (0, 1):
                x_copy(g, e, way).wait_send()
        for which in range(11):
            c_copy(g, which).wait()
        return 0

    for body in (first, second, third, last):
        lax.fori_loop(0, GROUPS, body, 0)
    own.wait()
    own_small.wait()
    for copy in small_copies:
        copy.wait()


def gather(pk, small):
    any_space = pl.BlockSpec(memory_space=pl.ANY)
    dma = pltpu.SemaphoreType.DMA
    return pl.pallas_call(
        gather_kernel,
        out_shape=(
            jax.ShapeDtypeStruct((UNITS, 8, 128, 1024), BF16),
            jax.ShapeDtypeStruct((8, 16, 128), BF16),
        ),
        in_specs=[any_space, any_space],
        out_specs=(any_space, any_space),
        scratch_shapes=[
            dma((2,)),
            dma((GROUPS, 3)),
            dma((GROUPS, 3)),
            dma((GROUPS, 4, 2)),
            dma((GROUPS, 4, 2)),
            dma((GROUPS, 11)),
            dma((GROUPS, 11)),
            dma((7,)),
            dma((7,)),
        ],
        compiler_params=pltpu.CompilerParams(collective_id=1, has_side_effects=True),
        name="gather_params",
    )(pk, small)


BLOCK = 256


def peers():
    fsdp, me = lax.axis_index("fsdp"), lax.axis_index("ctx")
    return me, [(lax.rem(me + d, 16), {"fsdp": fsdp, "ctx": lax.rem(me + d, 16)}) for d in range(1, 16)]


def exchange(src, dst, me, others, sends, recvs, local):
    copies = []
    for i, (other, device) in enumerate(others):
        copy = remote(src.at[other], dst.at[me], sends.at[i], recvs.at[i], device)
        copy.start()
        copies.append(copy)
    mine = pltpu.make_async_copy(src.at[me], dst.at[me], local)
    mine.start()
    mine.wait()
    for copy in copies:
        copy.wait()


def flipped(value):
    return value.astype(F32).T.astype(BF16)


def dot(a, b):
    return jnp.dot(a, b, preferred_element_type=F32)


def forward_kernel(send, got, o_t, log_total, mixed, k_all, q_t, v_t, o_send, a_s, a_r, b_s, b_r, local):
    me, others = peers()
    greet([device for _, device in others])
    exchange(send, got, me, others, a_s, a_r, local.at[0])

    def unpack(j, _):
        rows = pl.ds(pl.multiple_of(j * 192, 64), 192)
        k_all[rows, :] = got[j, 0:192, 64:128]
        return 0

    lax.fori_loop(0, 16, unpack, 0)
    for j in range(16):
        span = slice(j * 192, (j + 1) * 192)
        both = got[j, 0:192, :].astype(F32).T
        q_t[:, span] = both[0:64].astype(BF16)
        pair = got[j, 192:288, :].astype(F32).T
        v_t[0:64, span] = jnp.concatenate([pair[0:64], pair[64:128]], axis=1).astype(BF16)
    v_t[64:80, :] = jnp.ones((16, 3072), BF16)

    def block(i, _):
        span = pl.ds(pl.multiple_of(i * BLOCK, BLOCK), BLOCK)
        scores = dot(k_all[...], q_t[:, span])
        highest = jnp.max(scores, axis=0, keepdims=True)
        weights = jnp.exp(scores - highest).astype(BF16)
        out = dot(v_t[...], weights)
        total = out[64:65]
        o_t[:, span] = (out[0:64] / total).astype(BF16)
        log_total[:, span] = highest + jnp.log(total)
        return 0

    lax.fori_loop(0, 3072 // BLOCK, block, 0)
    for j in range(16):
        part = o_t[:, j * 192 : (j + 1) * 192].astype(F32)
        stacked = jnp.concatenate([part[:, 0:96], part[:, 96:192]], axis=0)
        o_send[j] = stacked.T.astype(BF16)
    exchange(o_send, mixed, me, others, b_s, b_r, local.at[1])


def forward_attention(send):
    vmem = pl.BlockSpec(memory_space=pltpu.VMEM)
    dma = pltpu.SemaphoreType.DMA
    return pl.pallas_call(
        forward_kernel,
        out_shape=(
            jax.ShapeDtypeStruct((16, 288, 128), BF16),
            jax.ShapeDtypeStruct((64, 3072), BF16),
            jax.ShapeDtypeStruct((1, 3072), F32),
            jax.ShapeDtypeStruct((16, 96, 128), BF16),
        ),
        in_specs=[vmem],
        out_specs=(vmem, vmem, vmem, vmem),
        scratch_shapes=[
            pltpu.VMEM((3072, 64), BF16),
            pltpu.VMEM((64, 3072), BF16),
            pltpu.VMEM((80, 3072), BF16),
            pltpu.VMEM((16, 96, 128), BF16),
            dma((15,)),
            dma((15,)),
            dma((15,)),
            dma((15,)),
            dma((2,)),
        ],
        compiler_params=pltpu.CompilerParams(collective_id=2, has_side_effects=True, vmem_limit_bytes=50 * MIB),
        name="attention_forward",
    )(send)


def backward_kernel(send, got, o_t, log_total, back, do_got, k_all, v_all, q_all, q_t, k_t, do_all, do_t, delta,
                    dq_t, dk, dv, out_send, a_s, a_r, b_s, b_r, local):
    me, others = peers()
    greet([device for _, device in others])
    exchange(send, do_got, me, others, a_s, a_r, local.at[0])
    for j in range(16):
        span = slice(j * 192, (j + 1) * 192)
        q_all[span, :] = got[j, 0:192, 0:64]
        k_all[span, :] = got[j, 0:192, 64:128]
        v_all[j * 192 : j * 192 + 96, :] = got[j, 192:288, 0:64]
        v_all[j * 192 + 96 : j * 192 + 192, :] = got[j, 192:288, 64:128]
        do_all[j * 192 : j * 192 + 96, :] = do_got[j, :, 0:64]
        do_all[j * 192 + 96 : j * 192 + 192, :] = do_got[j, :, 64:128]
        both = got[j, 0:192, :].astype(F32).T
        q_t[:, span] = both[0:64].astype(BF16)
        k_t[:, span] = both[64:128].astype(BF16)
        pair = do_got[j].astype(F32).T
        flat = jnp.concatenate([pair[0:64], pair[64:128]], axis=1)
        do_t[:, span] = flat.astype(BF16)
        delta[:, span] = jnp.sum(flat * o_t[:, span].astype(F32), axis=0, keepdims=True)
    dk[...] = jnp.zeros_like(dk)
    dv[...] = jnp.zeros_like(dv)

    def block(i, _):
        span = pl.ds(pl.multiple_of(i * BLOCK, BLOCK), BLOCK)
        prob = jnp.exp(dot(k_all[...], q_t[:, span]) - log_total[:, span])
        grad_prob = dot(v_all[...], do_t[:, span])
        dv[...] += dot(prob.astype(BF16), do_all[span, :])
        grad_scores = (prob * (grad_prob - delta[:, span])).astype(BF16)
        dk[...] += dot(grad_scores, q_all[span, :])
        dq_t[:, span] = dot(k_t[...], grad_scores) * 0.125
        return 0

    lax.fori_loop(0, 3072 // BLOCK, block, 0)
    for j in range(16):
        span = slice(j * 192, (j + 1) * 192)
        dq = dq_t[:, span].T
        out_send[j, 0:192, :] = jnp.concatenate([dq, dk[span, :]], axis=1).astype(BF16)
        out_send[j, 192:288, :] = jnp.concatenate(
            [dv[j * 192 : j * 192 + 96, :], dv[j * 192 + 96 : j * 192 + 192, :]], axis=1
        ).astype(BF16)
    exchange(out_send, back, me, others, b_s, b_r, local.at[1])


def backward_attention(send, got, o_t, log_total):
    vmem = pl.BlockSpec(memory_space=pltpu.VMEM)
    dma = pltpu.SemaphoreType.DMA
    return pl.pallas_call(
        backward_kernel,
        out_shape=jax.ShapeDtypeStruct((16, 288, 128), BF16),
        in_specs=[vmem] * 4,
        out_specs=vmem,
        scratch_shapes=[
            pltpu.VMEM((16, 96, 128), BF16),
            pltpu.VMEM((3072, 64), BF16),
            pltpu.VMEM((3072, 64), BF16),
            pltpu.VMEM((3072, 64), BF16),
            pltpu.VMEM((64, 3072), BF16),
            pltpu.VMEM((64, 3072), BF16),
            pltpu.VMEM((3072, 64), BF16),
            pltpu.VMEM((64, 3072), BF16),
            pltpu.VMEM((1, 3072), F32),
            pltpu.VMEM((64, 3072), F32),
            pltpu.VMEM((3072, 64), F32),
            pltpu.VMEM((3072, 64), F32),
            pltpu.VMEM((16, 288, 128), BF16),
            dma((15,)),
            dma((15,)),
            dma((15,)),
            dma((15,)),
            dma((2,)),
        ],
        compiler_params=pltpu.CompilerParams(collective_id=3, has_side_effects=True, vmem_limit_bytes=50 * MIB),
        name="attention_backward",
    )(send, got, o_t, log_total)


def reduce_kernel(n, *refs):
    units = refs[:n]
    sm = refs[n]
    out, sm_out = refs[n + 1 : n + 3]
    (acc, near, a_buf, b_buf, c_buf, final, s0, s1, s2, s3, l_s, n_s, n_r, a_s, a_r, b_s, b_r, c_s, c_r,
     d_s, d_r, e_s, e_r, t_s, t_r) = refs[n + 3 :]
    per = n // 3
    x, y, z, core = place()
    low, high = lax.rem(x, 2), x // 2
    at = (x, y, z)
    sibling = device_at(x, y, z, core + 1)
    mine = pl.ds(pl.multiple_of(core * 512, 512), 512)
    theirs = pl.ds(pl.multiple_of((1 - core) * 512, 512), 512)

    def line(axis, d):
        to = list(at)
        to[axis] = lax.rem(to[axis] + d, 4)
        return to[axis], device_at(*to, core)

    lines = [line(axis, d)[1] for axis in range(3) for d in (1, 2, 3)]
    plane = [device_at(x + a, y, z + d, core) for a in (0, 2) for d in range(4) if (a, d) != (0, 0)]
    greet([sibling] + lines + [plane[i] for i in (4, 5, 6)])

    t_copies = [remote(sm, s0, t_s.at[0], t_r.at[0], sibling)]
    t_copies[0].start()

    loads, nears = [], []
    order = [p * per + i for i in range(per) for p in range(3)]
    for u in order:
        copy = remote(units[u].at[:, :, :, :, :, theirs], near.at[u], n_s.at[u], n_r.at[u], sibling)
        copy.start()
        load = pltpu.make_async_copy(units[u].at[:, :, :, :, :, mine], acc.at[u], l_s.at[u])
        load.start()
        nears.append(copy)
        loads.append(load)
    for u, copy, load in zip(order, nears, loads):
        load.wait()
        copy.wait_recv()

        def pair(i, _, u=u):
            a, b = i // 4, lax.rem(i, 4)
            acc[u, a, b] = (acc[u, a, b].astype(F32) + near[u, a, b].astype(F32)).astype(BF16)
            return 0

        lax.fori_loop(0, 8, pair, 0)

    def part(ref, p):
        return ref.at[pl.ds(p * per, per)]

    def first_piece(p, c):
        whole = part(acc, p)
        if p == 0:
            return whole.at[:, lax.rem(c, 2), :, :, c // 2]
        if p == 1:
            return whole.at[:, :, c]
        return whole.at[:, :, :, c]

    def second_piece(p, ref, c):
        if p == 0:
            return ref.at[:, c]
        if p == 1:
            return ref.at[:, :, c]
        return ref.at[:, lax.rem(c, 2), :, c // 2]

    def third_piece(p, ref, c):
        if p == 0:
            return ref.at[:, c]
        if p == 1:
            return ref.at[:, lax.rem(c, 2), c // 2]
        return ref.at[:, c]

    def scatter(stage, pieces, bufs, sends, recvs):
        copies = []
        for d in (1, 3, 2):
            for p in range(3):
                axis = (p + stage) % 3
                c, device = line(axis, d)
                copy = remote(pieces[p](c), bufs[p].at[d - 1], sends.at[p, d - 1], recvs.at[p, d - 1], device)
                copy.start()
                copies.append(copy)
        return copies

    def add_up(stage, pieces, bufs):
        for p in range(3):
            axis = (p + stage) % 3
            own = pieces[p](at[axis])
            buf = bufs[p]

            def one(i, _, own=own, buf=buf):
                own[i] = (
                    own[i].astype(F32) + buf[0, i].astype(F32) + buf[1, i].astype(F32) + buf[2, i].astype(F32)
                ).astype(BF16)
                return 0

            lax.fori_loop(0, per, one, 0)

    a_bufs = list(a_buf)
    firsts = [functools.partial(first_piece, p) for p in range(3)]
    a_copies = scatter(0, firsts, a_bufs, a_s, a_r)

    def settle(buf, parts):
        total = parts[0]
        for other in parts[1:]:
            total = total + other
        return total

    t_copies[0].wait()
    s0[...] = s0[...] + sm[...]

    def small_stage(stage, axis, piece, buf):
        copies = []
        me = at[axis]
        for d in (1, 2, 3):
            c, device = line(axis, d)
            slot = 1 + 3 * stage + d - 1
            copies.append(remote(piece(c), buf.at[me], t_s.at[slot], t_r.at[slot], device))
            copies[-1].start()
        own = pltpu.make_async_copy(piece(me), buf.at[me], l_s.at[n + stage])
        own.start()
        own.wait()
        for copy in copies:
            copy.wait()

    small_stage(0, 1, lambda c: s0.at[:, c], s1)
    s0[:, 0] = s1[0] + s1[1] + s1[2] + s1[3]
    small_stage(1, 0, lambda c: s0.at[lax.rem(c, 2), 0], s2)
    s0[0, 1] = s2[0] + s2[1] + s2[2] + s2[3]
    small_stage(2, 2, lambda c: s0.at[0, 1], s3)
    sm_out[...] = s3[0] + s3[1] + s3[2] + s3[3]

    for copy in a_copies:
        copy.wait()
    add_up(0, firsts, a_bufs)

    def of(p, k):
        return firsts[p](at[p]) if k == 1 else second_piece(p, firsts[p](at[p]), at[(p + 1) % 3])

    seconds = [lambda c, p=p: second_piece(p, of(p, 1), c) for p in range(3)]
    b_bufs = list(b_buf)
    b_copies = scatter(1, seconds, b_bufs, b_s, b_r)
    for copy in b_copies:
        copy.wait()
    add_up(1, seconds, b_bufs)
    thirds = [lambda c, p=p: third_piece(p, of(p, 2), c) for p in range(3)]
    c_bufs = [c_buf.at[p] for p in range(3)]
    c_copies = scatter(2, thirds, c_bufs, c_s, c_r)
    for copy in c_copies:
        copy.wait()
    for p in range(3):
        own = thirds[p](at[(p + 2) % 3])
        for i in range(per):
            final[p * per + i] = (
                own[i].astype(F32)
                + c_buf[p, 0, i].astype(F32)
                + c_buf[p, 1, i].astype(F32)
                + c_buf[p, 2, i].astype(F32)
            ).astype(BF16)

    d_copies = []
    for i, device in enumerate(plane):
        copy = remote(final, out.at[:, z, high, :, mine], d_s.at[i], d_r.at[i], device)
        copy.start()
        d_copies.append(copy)
    own = pltpu.make_async_copy(final, out.at[:, z, high, :, mine], l_s.at[n + 3])
    own.start()
    own.wait()
    e_copies = [remote(final, out.at[:, z, high, :, mine], e_s.at[0], e_r.at[0], sibling)]
    e_copies[0].start()
    i = 0
    for a in (0, 2):
        for d in range(4):
            if (a, d) == (0, 0):
                continue
            d_copies[i].wait_recv()
            ref = out.at[:, lax.rem(z - d + 4, 4), lax.rem(high + a // 2, 2), :, mine]
            copy = remote(ref, ref, e_s.at[1 + i], e_r.at[1 + i], sibling)
            copy.start()
            e_copies.append(copy)
            i += 1
    for copy in nears + d_copies:
        copy.wait_send()
    for copy in e_copies:
        copy.wait()


def reduce(units, sm):
    n = len(units)
    per = n // 3
    any_space = pl.BlockSpec(memory_space=pl.ANY)
    vmem = pl.BlockSpec(memory_space=pltpu.VMEM)
    dma = pltpu.SemaphoreType.DMA
    return pl.pallas_call(
        functools.partial(reduce_kernel, n),
        out_shape=(
            jax.ShapeDtypeStruct((n, 4, 2, 16, 1024), BF16),
            jax.ShapeDtypeStruct((16, 128), F32),
        ),
        in_specs=[any_space] * n + [vmem],
        out_specs=(vmem, vmem),
        scratch_shapes=[
            pltpu.VMEM((n, 2, 4, 4, 2, 16, 512), BF16),
            pltpu.VMEM((n, 2, 4, 4, 2, 16, 512), BF16),
            (
                pltpu.VMEM((3, per, 4, 4, 16, 512), BF16),
                pltpu.VMEM((3, per, 2, 4, 2, 16, 512), BF16),
                pltpu.VMEM((3, per, 2, 4, 2, 16, 512), BF16),
            ),
            (
                pltpu.VMEM((3, per, 4, 16, 512), BF16),
                pltpu.VMEM((3, per, 2, 2, 16, 512), BF16),
                pltpu.VMEM((3, per, 4, 16, 512), BF16),
            ),
            pltpu.VMEM((3, 3, per, 16, 512), BF16),
            pltpu.VMEM((n, 16, 512), BF16),
            pltpu.VMEM((2, 4, 16, 128), F32),
            pltpu.VMEM((4, 2, 16, 128), F32),
            pltpu.VMEM((4, 16, 128), F32),
            pltpu.VMEM((4, 16, 128), F32),
            dma((n + 4,)),
            dma((n,)),
            dma((n,)),
            dma((3, 3)),
            dma((3, 3)),
            dma((3, 3)),
            dma((3, 3)),
            dma((3, 3)),
            dma((3, 3)),
            dma((7,)),
            dma((7,)),
            dma((8,)),
            dma((8,)),
            dma((10,)),
            dma((10,)),
        ],
        compiler_params=pltpu.CompilerParams(collective_id=4, has_side_effects=True, vmem_limit_bytes=58 * MIB),
        name="reduce_gradients",
    )(*[unit.reshape(2, 4, 4, 2, 16, 1024) for unit in units], sm)


def widened(values):
    return values.astype(F32)


def layer_norm(hidden, gain, offset):
    center = hidden - jnp.mean(hidden, axis=-1, keepdims=True)
    inverse = lax.rsqrt(jnp.mean(center * center, axis=-1, keepdims=True) + EPSILON)
    normed = center * inverse
    return (normed * gain + offset, normed, inverse)


def norm_back(upstream, normed, inverse, gain):
    scaled = upstream * gain
    return inverse * (
        scaled
        - jnp.mean(scaled, axis=-1, keepdims=True)
        - normed * jnp.mean(scaled * normed, axis=-1, keepdims=True)
    )


def gelu_value(inputs):
    return 0.5 * inputs * (1.0 + jax.scipy.special.erf(inputs * ROOT_HALF))


def gelu_slope(inputs):
    return (
        0.5 * (1.0 + jax.scipy.special.erf(inputs * ROOT_HALF))
        + inputs * jnp.exp(-0.5 * inputs * inputs) * INV_ROOT_TWO_PI
    )


def by_head(value):
    return value.reshape(-1, HEADS, HEAD_DIM).transpose(1, 0, 2)


def folded(value):
    half = value.shape[1] // 2
    return jnp.concatenate([value[:, :half], value[:, half:]], axis=2)


def unfolded(value):
    return jnp.concatenate([value[:, :, :HEAD_DIM], value[:, :, HEAD_DIM:]], axis=1)


def by_token(value):
    return value.transpose(1, 0, 2).reshape(-1, HEADS * HEAD_DIM)


def dot_nt(a, b):
    return lax.dot_general(a, b, (((1,), (1,)), ((), ())), preferred_element_type=F32)


def dot_tn(a, b):
    return lax.dot_general(a, b, (((0,), (0,)), ((), ())), preferred_element_type=F32)


def shards(layer_input, cotangent, w_qkv, b_q, b_v, w_out, b_out, g_attn, beta_attn, w_in, b_in, w_back, b_back,
           g_mlp, beta_mlp):
    width = layer_input.shape[-1]
    scale = 1.0 / math.sqrt(HEAD_DIM)
    in_units = w_in.reshape(128, 8, 4, 128).transpose(2, 0, 1, 3).reshape(4, 128, width)
    pk = jnp.concatenate(
        [w_qkv.reshape(128, 3, width).transpose(1, 0, 2), w_out[None], in_units, w_back.reshape(4, 128, width)]
    )
    small = jnp.concatenate(
        [jnp.stack([b_q, b_v, b_out, g_attn, beta_attn, b_back, g_mlp, beta_mlp]), b_in.reshape(4, 128),
         jnp.zeros((4, 128), BF16)]
    )
    full, smalls = gather(pk, small)
    full = full.reshape(UNITS, width, width)
    smalls = widened(smalls.transpose(1, 0, 2).reshape(16, width))
    bq, bv, bout, gattn, battn, bback, gmlp, bmlp = (smalls[i] for i in range(8))
    bin_ = [smalls[8 + j] for j in range(4)]

    rows = layer_input.reshape(-1, width)
    rows_low = rows.astype(BF16)
    query = ((dot(rows_low, full[0]) + bq) * scale).astype(BF16)
    keys = dot(rows_low, full[1]).astype(BF16)
    values = (dot(rows_low, full[2]) + bv).astype(BF16)
    send = jnp.concatenate(
        [jnp.concatenate([by_head(query), by_head(keys)], axis=2), folded(by_head(values))], axis=1
    )
    got, o_t, log_total, mixed_got = forward_attention(send)
    mixed = by_token(unfolded(mixed_got))

    first_sum = rows + dot(mixed, full[3]) + bout
    first_out, first_normed, first_inverse = layer_norm(first_sum, gattn, battn)
    first_low = first_out.astype(BF16)
    pre_act = [dot(first_low, full[4 + j]) + bin_[j] for j in range(4)]
    activated = [gelu_value(value).astype(BF16) for value in pre_act]
    second_sum = first_out + bback
    for j in range(4):
        second_sum = second_sum + dot(activated[j], full[8 + j])
    output, second_normed, second_inverse = layer_norm(second_sum, gmlp, bmlp)

    upstream = cotangent.reshape(-1, width)
    grad_g_mlp = jnp.sum(upstream * second_normed, axis=0)
    grad_beta_mlp = jnp.sum(upstream, axis=0)
    grad_second = norm_back(upstream, second_normed, second_inverse, gmlp)
    grad_b_back = jnp.sum(grad_second, axis=0)
    grad_second_low = grad_second.astype(BF16)
    grad_w_back = [dot_tn(activated[j], grad_second_low).astype(BF16) for j in range(4)]
    grad_pre = [dot_nt(grad_second_low, full[8 + j]) * gelu_slope(pre_act[j]) for j in range(4)]
    grad_b_in = [jnp.sum(value, axis=0) for value in grad_pre]
    grad_pre_low = [value.astype(BF16) for value in grad_pre]
    grad_w_in = [dot_tn(first_low, grad_pre_low[j]).astype(BF16) for j in range(4)]
    grad_first_out = grad_second
    for j in range(4):
        grad_first_out = grad_first_out + dot_nt(grad_pre_low[j], full[4 + j])
    grad_g_attn = jnp.sum(grad_first_out * first_normed, axis=0)
    grad_beta_attn = jnp.sum(grad_first_out, axis=0)
    grad_first = norm_back(grad_first_out, first_normed, first_inverse, gattn)
    grad_b_out = jnp.sum(grad_first, axis=0)
    grad_first_low = grad_first.astype(BF16)
    grad_w_out = dot_tn(mixed, grad_first_low).astype(BF16)
    grad_mixed = dot_nt(grad_first_low, full[3]).astype(BF16)

    back = backward_attention(folded(by_head(grad_mixed)), got, o_t, log_total)
    grad_query = by_token(back[:, :192, :HEAD_DIM])
    grad_keys = by_token(back[:, :192, HEAD_DIM:])
    grad_values = by_token(unfolded(back[:, 192:]))
    grad_b_q = jnp.sum(widened(grad_query), axis=0)
    grad_b_v = jnp.sum(widened(grad_values), axis=0)
    grad_w_qkv = [dot_tn(rows_low, value).astype(BF16) for value in (grad_query, grad_keys, grad_values)]
    grad_input = grad_first
    for i, value in enumerate((grad_query, grad_keys, grad_values)):
        grad_input = grad_input + dot_nt(value, full[i])

    sm = jnp.stack(
        [grad_b_q, grad_b_v, grad_b_out, grad_g_attn, grad_beta_attn, grad_b_back, grad_g_mlp, grad_beta_mlp]
        + grad_b_in
        + [jnp.zeros((width,), F32)] * 4
    )
    sm = sm.reshape(16, 8, 128).transpose(1, 0, 2).reshape(2, 4, 16, 128)
    owned, own_small = reduce(grad_w_qkv + [grad_w_out] + grad_w_in + grad_w_back, sm)
    owned = widened(owned.reshape(UNITS, 128, width))
    o_qkv = owned[0:3].transpose(1, 0, 2).reshape(128, 3 * width)
    o_in = owned[4:8].reshape(4, 128, 8, 128).transpose(1, 2, 0, 3).reshape(128, 4 * width)
    o_back = owned[8:12].reshape(512, width)
    return (
        output.reshape(layer_input.shape),
        grad_input.reshape(layer_input.shape),
        o_qkv,
        own_small[0],
        own_small[1],
        owned[3],
        own_small[2],
        own_small[3],
        own_small[4],
        o_in,
        own_small[8:12].reshape(512),
        o_back,
        own_small[5],
        own_small[6],
        own_small[7],
    )


def solution(mesh):
    big, mat, vec = P("fsdp", "ctx", None), P("fsdp", None), P("fsdp")
    params = (mat, vec, vec, mat, vec, vec, vec, mat, vec, mat, vec, vec, vec)
    return jax.shard_map(
        shards, mesh=mesh, in_specs=(big, big) + params, out_specs=(big, big) + params, check_vma=False
    )
```

time: 1620 us -> 487 us (0.30)
  waiting for transfers between devices: 743 us -> 0 us
  Pallas kernels: 0 us -> 333 us
  matrix products: 273 us -> 57.8 us
  blocking collectives: 186 us -> 0 us
  starting transfers between devices: 175 us -> 0 us
  other arithmetic: 128 us -> 10.5 us
    pallas_call x0 -> x4, Pallas kernels: none -> 333 us  [the longest x1 120 us: reduce(): pl.pallas_call(functools.partial(reduce_kernel, n), out_shape=(jax.ShapeD...]
    all_gather x6 -> x0, waiting for transfers between devices: 231 us -> none  [the longest x1 85.3 us: shards(): lax.all_gather(params[9], 'fsdp', axis=0, tiled=True)]
    reduce_scatter x3 -> x0, waiting for transfers between devices: 230 us -> none  [the longest x1 99 us: shards(): lax.psum_scatter(gradients[9].astype(jnp.bfloat16), 'fsdp', scatter_dimen...]
    dot_general x94 -> x36, matrix products: 273 us -> 57.8 us  [the longest x12 25.1 us: dot_tn(): lax.dot_general(a, b, (((0,), (0,)), ((), ())), preferred_element_type=F32)]
    ppermute x64 -> x0, starting transfers between devices: 174 us -> none  [passed_along(): return lax.ppermute(value, axis, pairs)]
    ppermute x64 -> x0, waiting for transfers between devices: 133 us -> none  [passed_along(): return lax.ppermute(value, axis, pairs)]
    all_gather x9 -> x0, blocking collectives: 121 us -> none  [the longest x1 19.5 us: shards(): lax.all_gather(params[8], 'fsdp', axis=0, tiled=True)]
    convert_element_type x86 -> x4, other arithmetic: 106 us -> 0.31 us  [the longest x1 0.21 us: shards(): first_low = first_out.astype(BF16)]
  transfers between devices with their start and end apart: 75 -> 0, of which waited for: 44 -> 0; matrix products, arithmetic and copies ran while one was open for 15% -> 0% of each run, Pallas kernels for 0% -> 0%
where the time goes in v1:
time: 487 us; the launch traced here: 478 us
  Pallas kernels  333 us (68%)
  local copies, waits for them, and re-layouts  74.7 us (15%)
  matrix products  57.8 us (12%)
  other arithmetic  10.5 us (2%)
    pallas_call x1, Pallas kernels, reduce(): pl.pallas_call(functools.partial(reduce_kernel, n), out_shape=(jax.ShapeD...  120 us
    pallas_call x1, Pallas kernels, gather(): pl.pallas_call(gather_kernel, out_shape=(jax.ShapeDtypeStruct((UNITS, 8,...  104 us
    pallas_call x1, Pallas kernels, backward_attention(): pl.pallas_call(backward_kernel, out_shape=jax.ShapeDtypeStruct((16, 288,...  55 us
    pallas_call x1, Pallas kernels, forward_attention(): pl.pallas_call(forward_kernel, out_shape=(jax.ShapeDtypeStruct((16, 288,...  54 us
    dot_general x12, matrix products, dot_tn(): lax.dot_general(a, b, (((0,), (0,)), ((), ())), preferred_element_type=F32)  25.1 us
    dot_general x12, matrix products, dot_nt(): lax.dot_general(a, b, (((1,), (1,)), ((), ())), preferred_element_type=F32)  17.3 us
    slice x1, local copies, waits for them, and re-layouts, shards(): pre_act = [dot(first_low, full[4 + j]) + bin_[j] for j in range(4)]  16.6 us
    dot_general x12, matrix products, dot(): return jnp.dot(a, b, preferred_element_type=F32)  15.4 us

profile of v1, /device:TPU:1, one launch (start us, length us, event | category | flops | bytes accessed | tf_op | source)
XLA Modules:
  0.0 478.0 jit_solution(1086002337202782984)
XLA Ops:
  5.1 2.9 pad_maximum_fusion.pk
  9.3 103.7 %gather_params.1 = (bf16[12,8,128,1024]{3,2,1,0:T(8,128)(2,1)}, bf16[8,16,128]{2,1,0:T(8,128)(2,1)}) custom-call(bf16[12,128,1024]{2,1,0:T(8,128)(2,1)} %pad_maximum_fusion.pk, bf16[16,128]{1,0:T(8,128)(2,1)} %concatenate.26.small), custom_call_target="tpu_custom_call" | custom-call | tf_op jit(solution)/shard_map/gather_params/pallas_call | solution.py:139
  113.0 16.6 %fusion.45 = (bf16[1,8,128,1024]{3,2,1,0:T(8,128)(2,1)}, bf16[1,8,128,1024]{3,2,1,0:T(8,128)(2,1)}, bf16[1,8,128,1024]{3,2,1,0:T(8,128)(2,1)}, bf16[1,8,128,1024...) fusion(bf16[12,8,128,1024]{3,2,1,0:T(8,128)(2,1)} %get-tuple-el, ...), kind=kLoop, calls=%fused_computation.136 | loop fusion | bytes 50331648 | tf_op jit(solution)/shard_map/slice | solution.py:663
  129.8 3.7 fusion.7
  135.5 2.2 copy.41
  137.7 2.0 fusion.49
  139.7 2.9 fusion.5
  142.7 2.0 copy.36
  144.6 2.2 copy.37
  151.6 54.0 %attention_forward.1 = (bf16[16,288,128]{2,1,0:T(8,128)(2,1)S(1)}, bf16[64,3072]{1,0:T(8,128)(2,1)S(1)}, f32[1,3072]{1,0:T(1,128)S(1)}, bf16[16,96,128]{2,1,0:T(8,128)(2,1)S(1)}) custom-call(bf16[16,288,128]{2,1,0:T(8,128)(2,1)S(1)} %maximum_maximum_fusion.send), custom_call_target="tpu_custom_call" | custom-call | tf_op jit(solution)/shard_map/attention_forward/pallas_call | solution.py:233
  208.3 2.5 fusion.52
  241.2 55.0 %attention_backward.1 = bf16[16,288,128]{2,1,0:T(8,128)(2,1)S(1)} custom-call(bf16[16,96,128]{2,1,0:T(8,128)(2,1)S(1)} %pad_maximum_fusion.1.send, bf16[16,288,128]{2,1,0:T(8,128)(2,1)S(1)} %get-tuple-element.26.got, bf16[64,3072]{1,0:T(8,128)(2,1)S(1)} %get-tuple-element.27.o_t, f32[1,3072]{1,0:T(1,128)S(1)} %get-tuple-element.28.log_total), custom_call_target="tpu_custom_call" | custom-call | tf_op jit(solution)/shard_map/attention_backward/pallas_call | solution.py:306
  299.7 2.7 stack.87
  302.4 2.1 convolution_convert_fusion
  304.5 2.2 convolution_convert_fusion.1
  306.7 2.1 convolution_convert_fusion.2
  308.8 2.2 convolution_convert_fusion.3
  311.0 2.1 convolution_convert_fusion.4
  313.1 2.1 convolution_convert_fusion.5
  315.1 2.1 convolution_convert_fusion.6
  317.2 2.1 convolution_convert_fusion.7
  319.4 2.0 convolution_convert_fusion.8
  322.4 2.1 convolution_convert_fusion.9
  327.1 2.1 convolution_convert_fusion.11
  329.6 2.1 convolution_convert_fusion.10
  331.6 120.3 %reduce_gradients.1 = (bf16[12,4,2,16,1024]{4,3,2,1,0:T(8,128)(2,1)}, f32[16,128]{1,0:T(8,128)}) custom-call(bf16[2,4,4,2,16,1024]{5,4,3,2,1,0:T(8,128)(2,1)} %bitcast.258, bf16[2,4,4,2,16,1024]{5,4,3,2,1,0:T(8,128)(2,1)} %bitcast.259, bf16[2,4,4,2,16,1024]{5,4,3,2,1,0:T(8,128)(2,1)} %bitcast.257, bf16[2,4,4,2,16,1024]{5,4,3,2,1,0:T(8,128)(2,1)} %bitcast.260, ...), custom_call_target="tpu_custom_call" | custom-call | tf_op jit(solution)/shard_map/reduce_gradients/pallas_call | solution.py:527
  452.0 3.3 fusion.46
  455.9 2.7 copy.49
  458.5 3.2 reshape.303
  463.1 3.0 copy.48
  466.1 3.0 copy.50
  471.1 2.9 convolution_add_fusion.4
  (197 shorter events, 59.8 us)
Async XLA Ops:
  5.0 3.1 copy-start.53
  5.0 3.0 copy-start.54
  5.0 3.0 copy-start.55
  5.0 3.0 copy-start.56
  5.0 3.0 copy-start.57
  5.0 3.0 copy-start.58
  5.0 3.0 copy-start.59
  5.0 3.0 copy-start.60
  5.1 3.0 copy-start.61
  113.0 16.6 %copy-start.50 = (bf16[8,16,128]{2,1,0:T(8,128)(2,1)S(1)}, bf16[8,16,128]{2,1,0:T(8,128)(2,1)}, u32[]{:S(2)}) copy-start(bf16[8,16,128]{2,1,0:T(8,128)(2,1)} %get-tuple-element.24) | copy-start | bytes 98308
  113.0 16.7 %copy-start.34 = (f32[1,192,1024]{2,1,0:T(8,128)S(1)}, f32[1,192,1024]{2,1,0:T(8,128)}, u32[]{:S(2)}) copy-start(f32[1,192,1024]{2,1,0:T(8,128)} %param.15) | copy-start | bytes 2359300
  129.7 17.2 %copy-start.1 = (bf16[1,8,128,1024]{3,2,1,0:T(8,128)(2,1)}, bf16[1,8,128,1024]{3,2,1,0:T(8,128)(2,1)S(1)}, u32[]{:S(2)}) copy-start(bf16[1,8,128,1024]{3,2,1,0:T(8,128)(2,1)S(1)} %get-tuple-element.67) | copy-start | bytes 6291460
  129.8 17.1 %copy-start.10 = (bf16[1,192,1024]{2,1,0:T(8,128)(2,1)}, bf16[1,192,1024]{2,1,0:T(8,128)(2,1)S(1)}, u32[]{:S(2)}) copy-start(bf16[1,192,1024]{2,1,0:T(8,128)(2,1)S(1)} %convert_element_type.129) | copy-start | bytes 1179652
  208.3 2.6 copy-start.27
  208.3 3.0 copy-start
  211.9 12.9 %copy-start.17 = (f32[192,1024]{1,0:T(8,128)}, f32[192,1024]{1,0:T(8,128)S(1)}, u32[]{:S(2)}) copy-start(f32[192,1024]{1,0:T(8,128)S(1)} %convolution_add_fusion.10) | copy-start | bytes 2359300
  213.3 13.2 %copy-start.23 = (f32[192,1024]{1,0:T(8,128)}, f32[192,1024]{1,0:T(8,128)S(1)}, u32[]{:S(2)}) copy-start(f32[192,1024]{1,0:T(8,128)S(1)} %convolution_add_fusion.12) | copy-start | bytes 2359300
  214.6 13.6 %copy-start.25 = (f32[192,1024]{1,0:T(8,128)}, f32[192,1024]{1,0:T(8,128)S(1)}, u32[]{:S(2)}) copy-start(f32[192,1024]{1,0:T(8,128)S(1)} %convolution_add_fusion.14) | copy-start | bytes 2359300
  215.9 13.9 %copy-start.19 = (f32[192,1024]{1,0:T(8,128)}, f32[192,1024]{1,0:T(8,128)S(1)}, u32[]{:S(2)}) copy-start(f32[192,1024]{1,0:T(8,128)S(1)} %convolution_add_fusion.16) | copy-start | bytes 2359300
  226.5 7.5 %copy-start.41 = (bf16[192,1024]{1,0:T(8,128)(2,1)}, bf16[192,1024]{1,0:T(8,128)(2,1)S(1)}, u32[]{:S(2)}) copy-start(bf16[192,1024]{1,0:T(8,128)(2,1)S(1)} %get-tuple-element.114) | copy-start | bytes 1179652
  228.2 5.0 %copy-start.43 = (bf16[192,1024]{1,0:T(8,128)(2,1)}, bf16[192,1024]{1,0:T(8,128)(2,1)S(1)}, u32[]{:S(2)}) copy-start(bf16[192,1024]{1,0:T(8,128)(2,1)S(1)} %get-tuple-element.112) | copy-start | bytes 1179652
  229.8 2.5 copy-start.45
  296.2 2.8 copy-start.22
  296.2 3.5 copy-start.51
  296.2 6.2 %copy-start.18 = (f32[192,1024]{1,0:T(8,128)S(1)}, f32[192,1024]{1,0:T(8,128)}, u32[]{:S(2)}) copy-start(f32[192,1024]{1,0:T(8,128)} %copy-done.17) | copy-start | bytes 2359300
  299.0 5.5 %copy-start.24 = (f32[192,1024]{1,0:T(8,128)S(1)}, f32[192,1024]{1,0:T(8,128)}, u32[]{:S(2)}) copy-start(f32[192,1024]{1,0:T(8,128)} %copy-done.23) | copy-start | bytes 2359300
  321.9 3.7 copy-start.29
  329.5 122.4 %copy-start.32 = (bf16[192,16,64]{0,2,1:T(8,128)(2,1)}, bf16[192,16,64]{0,2,1:T(8,128)(2,1)S(1)}, u32[]{:S(2)}) copy-start(bf16[192,16,64]{0,2,1:T(8,128)(2,1)S(1)} %copy.46) | copy-start | bytes 1179652
  458.5 3.2 copy-start.7
  466.1 3.9 copy-start.52
  471.1 2.9 copy-start.2
  471.1 2.9 copy-start.33
  (30 other events, 52.7 us)
